TPU v7x, 128 devices: a whole 4x4x4 slice. The times are simulated.
128 devices in a mesh: dp: 16 (over x, z), ctx: 8 (over y, core).
Axes of the slice: x: 4, y: 4, z: 4, core: 2. Of those that a mesh axis runs over, the one named last changes fastest.
Arguments:
- query_rows: bfloat16 [16, 1024, 8192], P('dp', 'ctx'), may hold values from -5 to 5
- key_rows: bfloat16 [16, 1024, 1024], P('dp', 'ctx'), may hold values from -5 to 5
- value_rows: bfloat16 [16, 1024, 1024], P('dp', 'ctx'), may hold values from -6 to 6
- layer_input: bfloat16 [16, 1024, 4096], P('dp', 'ctx'), may hold values from -6 to 6
- out_grad: bfloat16 [16, 1024, 8192], P('dp', 'ctx'), may hold values from -6 to 6
- parents: int32 [16, 8], P('dp'), may hold values from 0 to 7, as said below
- labels: int32 [16, 8], P('dp'), may hold values from 0 to 2
Outputs:
- attention_out: bfloat16 [16, 1024, 8192], P('dp', 'ctx')
- query_grad: bfloat16 [16, 1024, 8192], P('dp', 'ctx')
- key_grad: bfloat16 [16, 1024, 1024], P('dp', 'ctx')
- value_grad: bfloat16 [16, 1024, 1024], P('dp', 'ctx')
- value_weight_grad: float32 [4096, 1024], P(('dp', 'ctx'))
Inputs may be any that keep to these rules, and one draw needn't show every extreme that they name: parents[r, b] <= b for every block b; an entry equal to its own block starts a tree; blocks 0 and 7 always start trees.
All inputs are finite; a program needn't handle non-finite values.
Results may differ from a plain program's by a relative error of at most 0.024.
Values may be sent and summed in bfloat16 or wider, within the bound.
No kernel may reach another device: no remote copies, remote signals or barrier semaphores. Data moves between devices by JAX's collectives and lax.ppermute only.
A program may use at most 128 MiB of HBM per device.

v0:
```python
import jax
import jax.numpy as jnp
from jax import lax
from jax.sharding import PartitionSpec as P

HD = 128
BLK = 128


def block_reach(parent_row):
    total_blocks = parent_row.shape[0]
    block_ids = jnp.arange(total_blocks, dtype=jnp.int32)

    def advance(turn_index, carried):
        ancestry, current = carried
        matched = current[:, None] == block_ids[None, :]
        ancestry = ancestry | matched
        current = jnp.sum(jnp.where(matched, parent_row[None, :], 0), axis=1)
        return (ancestry, current)

    start_reach = jnp.zeros((total_blocks, total_blocks), dtype=bool)
    ancestry, current = lax.fori_loop(0, total_blocks, advance, (start_reach, block_ids))
    return ancestry


def per_device(query_rows, key_rows, value_rows, layer_input, out_grad, parents, labels):
    tok_local = query_rows.shape[1]
    ctx_count = lax.axis_size("ctx")
    seq_len = tok_local * ctx_count
    first_row = lax.axis_index("ctx") * tok_local
    positions = first_row + jnp.arange(tok_local, dtype=jnp.int32)
    total_blocks = labels.shape[1]
    block_ids = jnp.arange(total_blocks, dtype=jnp.int32)
    own_block = (positions // BLK)[:, None] == block_ids[None, :]
    own_label = jnp.sum(jnp.where(own_block, labels[0][None, :], 0), axis=1)
    sign_rows = jnp.where(own_label == 2, -1.0, 1.0).astype(jnp.float32)
    signed_grad = (out_grad[0].astype(jnp.float32) * sign_rows[:, None]).astype(jnp.bfloat16)
    ancestry = block_reach(parents[0])
    score_scale = HD ** (-0.5)
    query_full, key_full, value_full, grad_full = (
        lax.all_to_all(query_rows[0], "ctx", split_axis=1, concat_axis=0, tiled=True),
        lax.all_to_all(key_rows[0], "ctx", split_axis=1, concat_axis=0, tiled=True),
        lax.all_to_all(value_rows[0], "ctx", split_axis=1, concat_axis=0, tiled=True),
        lax.all_to_all(signed_grad, "ctx", split_axis=1, concat_axis=0, tiled=True),
    )
    wide_mask = jnp.broadcast_to(
        ancestry[:, None, :, None], (total_blocks, BLK, total_blocks, BLK)
    ).reshape(seq_len, seq_len)
    row_pos = lax.broadcasted_iota(jnp.int32, (seq_len, seq_len), 0)
    col_pos = lax.broadcasted_iota(jnp.int32, (seq_len, seq_len), 1)
    allowed = wide_mask & (col_pos <= row_pos)
    heads_here = query_full.shape[1] // HD

    def one_head(head_index, buffers):
        out_buf, query_buf, key_acc, value_acc = buffers
        col_query = head_index * HD
        query_head = lax.dynamic_slice_in_dim(query_full, col_query, HD, 1)
        grad_head = lax.dynamic_slice_in_dim(grad_full, col_query, HD, 1)
        scores = (
            jnp.einsum("sd,td->st", query_head, key_full, preferred_element_type=jnp.float32)
            * score_scale
        )
        scores = jnp.where(allowed, scores, -jnp.inf)
        row_max = jnp.max(scores, axis=1, keepdims=True)
        shifted = jnp.exp(scores - row_max)
        weights = shifted / jnp.sum(shifted, axis=1, keepdims=True)
        weights_low = weights.astype(jnp.bfloat16)
        head_out = jnp.dot(weights_low, value_full, preferred_element_type=jnp.float32).astype(
            jnp.bfloat16
        )
        grad_weights = jnp.einsum(
            "sd,td->st", grad_head, value_full, preferred_element_type=jnp.float32
        )
        inner_sum = jnp.sum(
            grad_head.astype(jnp.float32) * head_out.astype(jnp.float32), axis=1, keepdims=True
        )
        grad_scores = (weights * (grad_weights - inner_sum) * score_scale).astype(jnp.bfloat16)
        head_dq = jnp.dot(grad_scores, key_full, preferred_element_type=jnp.float32).astype(
            jnp.bfloat16
        )
        head_dk = jnp.einsum(
            "st,sd->td", grad_scores, query_head, preferred_element_type=jnp.float32
        )
        head_dv = jnp.einsum(
            "st,sd->td", weights_low, grad_head, preferred_element_type=jnp.float32
        )
        out_buf = lax.dynamic_update_slice_in_dim(out_buf, head_out, col_query, 1)
        query_buf = lax.dynamic_update_slice_in_dim(query_buf, head_dq, col_query, 1)
        key_old = key_acc
        key_acc = key_old + head_dk
        value_old = value_acc
        value_acc = value_old + head_dv
        return (out_buf, query_buf, key_acc, value_acc)

    start_buffers = (
        jnp.zeros(query_full.shape, jnp.bfloat16),
        jnp.zeros(query_full.shape, jnp.bfloat16),
        jnp.zeros(key_full.shape, jnp.float32),
        jnp.zeros(key_full.shape, jnp.float32),
    )
    out_buf, query_buf, key_acc, value_acc = lax.fori_loop(0, heads_here, one_head, start_buffers)
    key_grad_heads = key_acc.astype(jnp.bfloat16)
    value_grad_heads = value_acc.astype(jnp.bfloat16)
    out_local, query_local, key_local, value_local = (
        lax.all_to_all(out_buf, "ctx", split_axis=0, concat_axis=1, tiled=True),
        lax.all_to_all(query_buf, "ctx", split_axis=0, concat_axis=1, tiled=True),
        lax.all_to_all(key_grad_heads, "ctx", split_axis=0, concat_axis=1, tiled=True),
        lax.all_to_all(value_grad_heads, "ctx", split_axis=0, concat_axis=1, tiled=True),
    )
    grad_norm = (seq_len * lax.axis_size("dp")) ** (-0.5)
    input_cols = layer_input[0]
    weight_grad = lax.psum_scatter(
        jnp.einsum("tr,tc->rc", input_cols, value_local, preferred_element_type=jnp.float32),
        ("dp", "ctx"),
        scatter_dimension=0,
        tiled=True,
    )
    weight_grad = weight_grad * grad_norm
    return (out_local[None], query_local[None], key_local[None], value_local[None], weight_grad)


def solution(mesh):
    placed = (
        P("dp", "ctx", None),
        P("dp", "ctx", None),
        P("dp", "ctx", None),
        P("dp", "ctx", None),
        P("dp", "ctx", None),
        P("dp", None),
        P("dp", None),
    )
    return jax.shard_map(
        per_device,
        mesh=mesh,
        in_specs=placed,
        out_specs=(
            P("dp", "ctx", None),
            P("dp", "ctx", None),
            P("dp", "ctx", None),
            P("dp", "ctx", None),
            P(("dp", "ctx"), None),
        ),
        check_vma=False,
    )
```

profile of v0, /device:TPU:1, one launch (start us, length us, event | category | flops | bytes accessed | tf_op | source)
XLA Modules:
  0.0 952.4 jit_solution(1654982712321087577)
XLA Ops:
  9.1 6.0 all-to-all-start.1
  17.6 2.9 copy.56
  21.7 5.0 all-to-all-start.2
  26.6 3.9 multiply_convert_fusion.1
  30.5 2.8 all-to-all-done.2
  33.3 4.5 all-to-all-start.3
  37.8 3.0 copy.78
  43.3 20.9 %all-to-all-done.3 = bf16[128,8,1024]{0,2,1:T(8,128)(2,1)S(1)} async-done(((bf16[128,8,1024]{0,2,1:T(8,128)(2,1)}), bf16[128,8,1024]{0,2,1:T(8,128)(2,1)S(1)}, u32[]{:S(2)}, u32[]{:S(2)}) %all-to-all-start.3) | async-done | bytes 2097184 | tf_op jit(solution)/shard_map/all_to_all | solution.py:44
  64.2 5.1 all-to-all-start
  74.2 21.5 %all-to-all-done = bf16[128,8,1024]{2,0,1:T(8,128)(2,1)} async-done(((bf16[128,8,1024]{2,0,1:T(8,128)(2,1)}), bf16[128,8,1024]{2,0,1:T(8,128)(2,1)}, u32[]{:S(2)}, u32[]{:S(2)}) %all-to-all-start) | async-done | bytes 2097184 | tf_op jit(solution)/shard_map/all_to_all | solution.py:41
  98.9 146.5 %while.34 = (s32[]{:T(128)}, bf16[1024,1024]{1,0:T(8,128)(2,1)}, bf16[1024,1024]{1,0:T(8,128)(2,1)}, f32[1024,128]{1,0:T(8,128)}, f32[1024,128]{1,0:T(8,128)}, /...) while((s32[]{:T(128)}, bf16[1024,1024]{1,0:T(8,128)(2,1)}, ...), condition=%wide.region_8.9_spmd.clone, body=%wide.region_4.8_spmd.clone.sunk | while | flops 1628697600 | bytes 38572312 | solution.py:101
  128.8 2.7 convolution_add_fusion.4
  147.2 2.7 convolution_add_fusion.4
  246.5 10.0 %all_to_all.140 = bf16[8,128,128]{2,1,0:T(8,128)(2,1)S(1)} all-to-all(bf16[8,128,128]{2,1,0:T(8,128)(2,1)S(1)} %bitcast.99), channel_id=1, replica_groups=mesh['dp'=16,'ctx'=8] {'ctx'}, dimensions={0} | all-to-all | bytes 524288 | tf_op jit(solution)/shard_map/all_to_all | solution.py:108
  256.6 8.0 convolution_bitcast_fusion
  264.6 17.4 %copy.72 = f32[4096,1024]{1,0:T(8,128)} copy(f32[4096,1024]{0,1:T(8,128)} %convolution_bitcast_fusion) | data formatting | bytes 33554432
  283.2 10.6 %all_to_all.141 = bf16[8,128,128]{2,1,0:T(8,128)(2,1)} all-to-all(bf16[8,128,128]{2,1,0:T(8,128)(2,1)S(1)} %bitcast.100), channel_id=1, replica_groups=mesh['dp'=16,'ctx'=8] {'ctx'}, dimensions={0} | all-to-all | bytes 524288 | tf_op jit(solution)/shard_map/all_to_all | solution.py:107
  293.8 36.5 %all_to_all.142 = bf16[8,128,1024]{2,1,0:T(8,128)(2,1)} all-to-all(bf16[8,128,1024]{2,1,0:T(8,128)(2,1)} %bitcast.92), channel_id=1, replica_groups=mesh['dp'=16,'ctx'=8] {'ctx'}, dimensions={0} | all-to-all | bytes 4194304 | tf_op jit(solution)/shard_map/all_to_all | solution.py:105
  330.3 4.2 all-to-all-start.5
  337.3 3.9 copy.62
  341.2 4.1 copy.66
  345.3 18.5 %all-to-all-done.5 = bf16[8,128,1024]{2,1,0:T(8,128)(2,1)S(1)} async-done(((bf16[8,128,1024]{2,1,0:T(8,128)(2,1)}), bf16[8,128,1024]{2,1,0:T(8,128)(2,1)S(1)}, u32[]{:S(2)}, u32[]{:S(2)}) %all-to-all-start.5) | async-done | bytes 2097184 | tf_op jit(solution)/shard_map/all_to_all | solution.py:106
  366.1 4.1 copy.67
  370.2 573.4 %reduce-scatter.4.cloned.1.call-done = f32[32,1024]{1,0:T(8,128)} async-done(((f32[4096,1024]{1,0:T(8,128)}), f32[32,1024]{1,0:T(8,128)}) %reduce-scatter.4.cloned.1.call-update) | async-done | bytes 131088
  (164 shorter events, 168.6 us)
Async XLA Ops:
  7.2 249.4 %copy-start = (bf16[1,128,4096]{2,1,0:T(8,128)(2,1)S(1)}, bf16[1,128,4096]{2,1,0:T(8,128)(2,1)}, u32[]{:S(2)}) copy-start(bf16[1,128,4096]{2,1,0:T(8,128)(2,1)} %param.14) | copy-start | bytes 3145732
  7.2 10.4 %copy-start.2 = (bf16[1,128,8192]{2,1,0:T(8,128)(2,1)S(1)}, bf16[1,128,8192]{2,1,0:T(8,128)(2,1)}, u32[]{:S(2)}) copy-start(bf16[1,128,8192]{2,1,0:T(8,128)(2,1)} %param.15) | copy-start | bytes 6291460
  9.1 12.6 %all-to-all-start.1 = ((bf16[128,8,128]{2,0,1:T(8,128)(2,1)}), bf16[128,8,128]{2,0,1:T(8,128)(2,1)}, u32[]{:S(2)}, u32[]{:S(2)}) async-start(bf16[128,8,128]{2,0,1:T(8,128)(2,1)} %copy.54), calls=%async_computation.1 | async-start | bytes 524288 | tf_op jit(solution)/shard_map/all_to_all | solution.py:42
  21.7 11.6 %all-to-all-start.2 = ((bf16[128,8,128]{2,0,1:T(8,128)(2,1)}), bf16[128,8,128]{2,0,1:T(8,128)(2,1)}, u32[]{:S(2)}, u32[]{:S(2)}) async-start(bf16[128,8,128]{2,0,1:T(8,128)(2,1)} %copy.55), calls=%async_computation.2 | async-start | bytes 524288 | tf_op jit(solution)/shard_map/all_to_all | solution.py:43
  33.3 30.9 %all-to-all-start.3 = ((bf16[128,8,1024]{0,2,1:T(8,128)(2,1)}), bf16[128,8,1024]{0,2,1:T(8,128)(2,1)S(1)}, u32[]{:S(2)}, u32[]{:S(2)}) async-start(bf16[128,8,1024]{0,2,1:T(8,128)(2,1)} %multiply_convert_fusion.1), calls=%async_computation.3 | async-start | bytes 4194304 | tf_op jit(solution)/shard_map/all_to_all | solution.py:44
  43.3 26.0 %copy-start.3 = (s32[1,8]{1,0:T(1,128)S(1)}, s32[1,8]{1,0:T(1,128)}, u32[]{:S(2)}) copy-start(s32[1,8]{1,0:T(1,128)} %param.16) | copy-start | bytes 100
  64.2 31.5 %all-to-all-start = ((bf16[128,8,1024]{2,0,1:T(8,128)(2,1)}), bf16[128,8,1024]{2,0,1:T(8,128)(2,1)}, u32[]{:S(2)}, u32[]{:S(2)}) async-start(bf16[128,8,1024]{2,0,1:T(8,128)(2,1)} %copy.53), calls=%async_computation | async-start | bytes 4194304 | tf_op jit(solution)/shard_map/all_to_all | solution.py:41
  69.2 874.3 %reduce-scatter.4.cloned.1.call-start = ((), (), s32[]{:S(2)}) async-start(), calls=%async_computation.9 | async-start | bytes 16908288
  282.1 1.0 copy-start.1
  330.3 33.4 %all-to-all-start.5 = ((bf16[8,128,1024]{2,1,0:T(8,128)(2,1)}), bf16[8,128,1024]{2,1,0:T(8,128)(2,1)S(1)}, u32[]{:S(2)}, u32[]{:S(2)}) async-start(bf16[8,128,1024]{2,1,0:T(8,128)(2,1)} %bitcast.91), calls=%async_computation.5 | async-start | bytes 4194304 | tf_op jit(solution)/shard_map/all_to_all | solution.py:106
Sparse Core Ops, SparseCore 0:
  282.2 661.3 reduce-scatter.3
where the time goes:
time: 961 us; the launch traced here: 952 us
  waiting for transfers between devices  638 us (66%)
  matrix products  117 us (12%)
  local copies, waits for them, and re-layouts  82 us (9%)
  blocking collectives  57.1 us (6%)
  starting transfers between devices  24.7 us (3%)
  other arithmetic  18.4 us (2%)
  between operations  14.1 us (1%)
    unnamed x2, waiting for transfers between devices  573 us
    all_to_all x1, blocking collectives, per_device(): lax.all_to_all(out_buf, 'ctx', split_axis=0, concat_axis=1, tiled=True)  36.5 us
    unnamed x19, local copies, waits for them, and re-layouts  35.5 us
    all_to_all x1, waiting for transfers between devices, per_device(): lax.all_to_all(query_rows[0], 'ctx', split_axis=1, concat_axis=0, tiled=T...  21.5 us
    dot_general x8, matrix products, one_head(): jnp.einsum('st,sd->td', grad_scores, query_head, preferred_element_type=j...  21.2 us
    all_to_all x1, waiting for transfers between devices, per_device(): lax.all_to_all(signed_grad, 'ctx', split_axis=1, concat_axis=0, tiled=True)  20.9 us
    dot_general x8, matrix products, one_head(): jnp.dot(grad_scores, key_full, preferred_element_type=jnp.float32)  19.5 us
    dot_general x8, matrix products, one_head(): jnp.einsum('st,sd->td', weights_low, grad_head, preferred_element_type=jn...  19.4 us
  transfers between devices with their start and end apart: 6, of which 6 were waited for; matrix products, arithmetic and copies ran while one was open for 4% of the time, Pallas kernels for 0%

commit v1 on v0

v1 whole, which is shorter than its diff:
```python
import functools

import jax
import jax.numpy as jnp
from jax import lax
from jax.experimental import pallas as pl
from jax.experimental.pallas import tpu as pltpu
from jax.sharding import PartitionSpec as P

HD = 128
BLK = 128
GRP = 8
NY = 4
NZ = 4
NX = 4
HALF = 4
CH = 1
PER = HALF // CH
QW = GRP * HD
SLOTS = 2 * NY
PAIRS = 4
LOW = jnp.bfloat16
F32 = jnp.float32
SCALE = HD**-0.5
EXP_SCALE = SCALE * 1.4426950408889634
MASKED = -1e30


def dot_nt(a, b):
    return lax.dot_general(a, b, (((1,), (1,)), ((), ())), preferred_element_type=F32)


def dot_nn(a, b):
    return lax.dot_general(a, b, (((1,), (0,)), ((), ())), preferred_element_type=F32)


def dot_tn(a, b):
    return lax.dot_general(a, b, (((0,), (0,)), ((), ())), preferred_element_type=F32)


def attention_kernel(
    place, parents, labels,
    q_own, q_par, g_own, g_par, kv0, kv1, kv2, kv3,
    o_own, o_par, dq_own, dq_par, dkv0, dkv1, dkv2, dkv3,
    chain, k_all, v_all, k_pair, v_pair, q_st, g_st, s_st, w_st, m_st, l_st, o_st, dq_st, dk_acc, dv_acc,
):
    y = place[0]
    c = place[1]
    for d, kv in enumerate((kv0, kv1, kv2, kv3)):
        for e in range(2):
            k_all[2 * d + e] = kv[0, e]
            v_all[2 * d + e] = kv[1, e]
    dk_acc[...] = jnp.zeros_like(dk_acc)
    dv_acc[...] = jnp.zeros_like(dv_acc)
    row = lax.broadcasted_iota(jnp.int32, (BLK, BLK), 0)
    col = lax.broadcasted_iota(jnp.int32, (BLK, BLK), 1)
    causal = jnp.where(col <= row, 0.0, MASKED).astype(F32)

    def slot_of(block):
        return 2 * (y - block // 2) + jnp.bitwise_xor(block % 2, c)

    def one_block(block, q_ref, g_ref, o_ref, dq_ref):
        def walk(step, carry):
            current, count = carry
            above = parents[0, current]
            more = above != current
            nxt = jnp.where(more, above, current)
            chain[step + 1] = slot_of(nxt)
            return nxt, count + more.astype(jnp.int32)

        chain[0] = slot_of(block)
        _, count = lax.fori_loop(0, SLOTS - 1, walk, (block, jnp.int32(1)))
        pairs = (count + 1) // 2
        sign = jnp.where(labels[0, block] == 2, -1.0, 1.0).astype(F32)

        for h in range(GRP):
            rows = slice(h * BLK, (h + 1) * BLK)
            cols = slice(h * HD, (h + 1) * HD)
            q_st[rows, :] = q_ref[:, cols]
            g_st[rows, :] = (g_ref[:, cols].astype(F32) * sign).astype(LOW)
        m_st[...] = jnp.full_like(m_st, MASKED)
        l_st[...] = jnp.zeros_like(l_st)
        o_st[...] = jnp.zeros_like(o_st)
        dq_st[...] = jnp.zeros_like(dq_st)

        def score(t, _):
            for e in range(2):
                s = chain[2 * t + e]
                k_pair[t, e * BLK : (e + 1) * BLK, :] = k_all[s]
                v_pair[t, e * BLK : (e + 1) * BLK, :] = v_all[s]
            left = jnp.where(t > 0, 0.0, causal)
            right = jnp.where(2 * t + 1 < count, 0.0, MASKED).astype(F32)
            for h in range(GRP):
                rows = slice(h * BLK, (h + 1) * BLK)
                s = dot_nt(q_st[rows, :], k_pair[t])
                s_l = s[:, :BLK] + left
                s_r = s[:, BLK:] + right
                s_st[t, rows, :BLK] = s_l
                s_st[t, rows, BLK:] = s_r
                m_st[rows, :] = jnp.maximum(m_st[rows, :], jnp.maximum(s_l, s_r))
            return 0

        lax.fori_loop(0, pairs, score, 0)
        for h in range(GRP):
            rows = slice(h * BLK, (h + 1) * BLK)
            m_st[rows, :] = jnp.broadcast_to(jnp.max(m_st[rows, :], axis=1, keepdims=True), (BLK, BLK))

        def expo(t, _):
            for h in range(GRP):
                rows = slice(h * BLK, (h + 1) * BLK)
                m = m_st[rows, :]
                p_l = jnp.exp2((s_st[t, rows, :BLK] - m) * EXP_SCALE)
                p_r = jnp.exp2((s_st[t, rows, BLK:] - m) * EXP_SCALE)
                s_st[t, rows, :BLK] = p_l
                s_st[t, rows, BLK:] = p_r
                l_st[rows, :] += p_l + p_r
            return 0

        lax.fori_loop(0, pairs, expo, 0)
        for h in range(GRP):
            rows = slice(h * BLK, (h + 1) * BLK)
            total = jnp.sum(l_st[rows, :], axis=1, keepdims=True)
            l_st[rows, :] = jnp.broadcast_to(1.0 / total, (BLK, BLK))

        def values(t, _):
            for h in range(GRP):
                rows = slice(h * BLK, (h + 1) * BLK)
                r = l_st[rows, :]
                w_l = s_st[t, rows, :BLK] * r
                w_r = s_st[t, rows, BLK:] * r
                s_st[t, rows, :BLK] = w_l
                s_st[t, rows, BLK:] = w_r
                w_st[rows, :BLK] = w_l.astype(LOW)
                w_st[rows, BLK:] = w_r.astype(LOW)
                o_st[rows, :] += dot_nn(w_st[rows, :], v_pair[t])
            dv = dot_tn(w_st[...], g_st[...])
            for e in range(2):
                dv_acc[chain[2 * t + e]] += dv[e * BLK : (e + 1) * BLK, :]
            return 0

        lax.fori_loop(0, pairs, values, 0)
        for h in range(GRP):
            rows = slice(h * BLK, (h + 1) * BLK)
            out = o_st[rows, :].astype(LOW)
            o_ref[:, h * HD : (h + 1) * HD] = out
            inner = jnp.sum(g_st[rows, :].astype(F32) * out.astype(F32), axis=1, keepdims=True)
            m_st[rows, :] = jnp.broadcast_to(inner, (BLK, BLK))

        def grads(t, _):
            for h in range(GRP):
                rows = slice(h * BLK, (h + 1) * BLK)
                inner = m_st[rows, :]
                dp = dot_nt(g_st[rows, :], v_pair[t])
                ds_l = s_st[t, rows, :BLK] * (dp[:, :BLK] - inner)
                ds_r = s_st[t, rows, BLK:] * (dp[:, BLK:] - inner)
                w_st[rows, :BLK] = ds_l.astype(LOW)
                w_st[rows, BLK:] = ds_r.astype(LOW)
                dq_st[rows, :] += dot_nn(w_st[rows, :], k_pair[t])
            dk = dot_tn(w_st[...], q_st[...])
            for e in range(2):
                dk_acc[chain[2 * t + e]] += dk[e * BLK : (e + 1) * BLK, :]
            return 0

        lax.fori_loop(0, pairs, grads, 0)
        for h in range(GRP):
            rows = slice(h * BLK, (h + 1) * BLK)
            dq_ref[:, h * HD : (h + 1) * HD] = (dq_st[rows, :] * SCALE).astype(LOW)

    one_block(2 * y + c, q_own, g_own, o_own, dq_own)
    one_block(2 * y + 1 - c, q_par, g_par, o_par, dq_par)
    for d, dkv in enumerate((dkv0, dkv1, dkv2, dkv3)):
        for e in range(2):
            dkv[0, e] = (dk_acc[2 * d + e] * SCALE).astype(LOW)
            dkv[1, e] = dv_acc[2 * d + e].astype(LOW)


def attention(chunk, place, parents, labels, q, q_par, g, g_par, kvs):
    own = pl.BlockSpec((BLK, QW), lambda i, place, par, lab: (0, place[1] * HALF + chunk * PER + i))
    par = pl.BlockSpec((BLK, QW), lambda i, place, par, lab: (0, i))
    own_out = pl.BlockSpec((BLK, QW), lambda i, place, par, lab: (0, place[1] * PER + i))
    kv = pl.BlockSpec((2, 2, BLK, HD), lambda i, place, par, lab: (0, 0, 0, i))
    own_shape = jax.ShapeDtypeStruct((BLK, 2 * PER * QW), LOW)
    par_shape = jax.ShapeDtypeStruct((BLK, PER * QW), LOW)
    kv_shape = jax.ShapeDtypeStruct((2, 2, BLK, PER * HD), LOW)
    rows = GRP * BLK
    return pl.pallas_call(
        attention_kernel,
        grid_spec=pltpu.PrefetchScalarGridSpec(
            num_scalar_prefetch=3,
            grid=(PER,),
            in_specs=[own, par, own, par, kv, kv, kv, kv],
            out_specs=[own_out, par, own_out, par, kv, kv, kv, kv],
            scratch_shapes=[
                pltpu.SMEM((SLOTS,), jnp.int32),
                pltpu.VMEM((SLOTS, BLK, HD), LOW),
                pltpu.VMEM((SLOTS, BLK, HD), LOW),
                pltpu.VMEM((PAIRS, 2 * BLK, HD), LOW),
                pltpu.VMEM((PAIRS, 2 * BLK, HD), LOW),
                pltpu.VMEM((rows, HD), LOW),
                pltpu.VMEM((rows, HD), LOW),
                pltpu.VMEM((PAIRS, rows, 2 * BLK), F32),
                pltpu.VMEM((rows, 2 * BLK), LOW),
                pltpu.VMEM((rows, BLK), F32),
                pltpu.VMEM((rows, BLK), F32),
                pltpu.VMEM((rows, HD), F32),
                pltpu.VMEM((rows, HD), F32),
                pltpu.VMEM((SLOTS, BLK, HD), F32),
                pltpu.VMEM((SLOTS, BLK, HD), F32),
            ],
        ),
        out_shape=[own_shape, par_shape, own_shape, par_shape, kv_shape, kv_shape, kv_shape, kv_shape],
        compiler_params=pltpu.CompilerParams(
            dimension_semantics=("arbitrary",), vmem_limit_bytes=32 * 2**20
        ),
        cost_estimate=pl.CostEstimate(
            flops=6 * 2 * PER * rows * 2 * 4 * BLK * HD,
            bytes_accessed=8 * BLK * PER * QW * 2,
            transcendentals=PER * rows * 2 * 4 * BLK,
        ),
        name="tree_attention",
    )(place, parents, labels, q, q_par, g, g_par, *kvs)


def device(x, z, y, c):
    return (x * NZ + z) * SLOTS + y * 2 + c


def per_device(query_rows, key_rows, value_rows, layer_input, out_grad, parents, labels):
    ctx = lax.axis_index("ctx")
    dp = lax.axis_index("dp")
    y, c, z = ctx // 2, ctx % 2, dp % NZ
    place = jnp.stack([y, c]).astype(jnp.int32)
    q, k, v, g, x = query_rows[0], key_rows[0], value_rows[0], out_grad[0], layer_input[0]

    def swap(a):
        return lax.ppermute(a, "ctx", [(i, i ^ 1) for i in range(SLOTS)])

    def later(a, d):
        return lax.ppermute(a, "ctx", [(i, i + 2 * d) for i in range(SLOTS - 2 * d)])

    def earlier(a, d):
        return lax.ppermute(a, "ctx", [(i + 2 * d, i) for i in range(SLOTS - 2 * d)])

    def along_z(a, d):
        return lax.ppermute(a, "dp", [(i, i // NZ * NZ + (i + d) % NZ) for i in range(NX * NZ)])

    def cols(a, start, width):
        return lax.dynamic_slice_in_dim(a, start, width, 1)

    o_chunks, dq_chunks, dk_chunks, dv_chunks = [], [], [], []
    kv_both = jnp.stack([k, v])
    for ch in range(CH):
        width = PER * HD
        mine = lax.dynamic_slice_in_dim(kv_both, c * HALF * HD + ch * width, width, 2)
        other = lax.dynamic_slice_in_dim(kv_both, (1 - c) * HALF * HD + ch * width, width, 2)
        kv = jnp.stack([mine, swap(other)], axis=1)
        kvs = [kv] + [later(kv, d) for d in range(1, NY)]
        at = (1 - c) * HALF * QW + ch * PER * QW
        q_par = swap(cols(q, at, PER * QW))
        g_par = swap(cols(g, at, PER * QW))
        o_own, o_par, dq_own, dq_par, *dkvs = attention(ch, place, parents, labels, q, q_par, g, g_par, kvs)
        total = dkvs[0].astype(F32)
        for d in range(1, NY):
            total = total + earlier(dkvs[d], d).astype(F32)
        total = total.astype(LOW)
        o_chunks.append(lax.dynamic_update_slice_in_dim(o_own, swap(o_par), (1 - c) * PER * QW, 1))
        dq_chunks.append(lax.dynamic_update_slice_in_dim(dq_own, swap(dq_par), (1 - c) * PER * QW, 1))
        dkv_other = swap(total[:, 1])
        dkv_own = total[:, 0]
        first = jnp.where(c == 0, dkv_own, dkv_other)
        second = jnp.where(c == 0, dkv_other, dkv_own)
        both = jnp.concatenate([first, second], axis=-1)
        dk_chunks.append(both[0])
        dv_chunks.append(both[1])
        dv_low = total[1].reshape(2 * BLK, width)

    parts = x.reshape(BLK, NX, NZ, -1)
    wide = NX * parts.shape[3]

    def rows_for(d):
        return lax.dynamic_index_in_dim(parts, (z + d) % NZ, 2, keepdims=False).reshape(BLK, wide)

    x_z = [rows_for(0)] + [along_z(rows_for(d), d) for d in range(1, NZ)]
    x_z = jnp.stack(x_z)
    x_all = jnp.stack([x_z, swap(x_z)], axis=1)
    dv_all = jnp.stack([dv_low] + [along_z(dv_low, d) for d in range(1, NZ)])
    partial = jnp.dot(
        x_all.reshape(NZ * 2 * BLK, wide).T, dv_all.reshape(NZ * 2 * BLK, -1), preferred_element_type=F32
    ).astype(LOW)
    groups = [
        [device(xx, zz, yy, cc) for xx in range(NX) for yy in range(NY)] for zz in range(NZ) for cc in range(2)
    ]
    share = partial.reshape(NX * NY, -1, partial.shape[1])
    share = lax.all_to_all(share, ("dp", "ctx"), 0, 0, axis_index_groups=groups)
    summed = jnp.sum(share.astype(F32), axis=0) * (16 * SLOTS * BLK) ** -0.5
    keep = lax.dynamic_slice_in_dim(summed, c * 32, 32, 0)
    gone = swap(lax.dynamic_slice_in_dim(summed, (1 - c) * 32, 32, 0))
    weight_grad = jnp.concatenate([jnp.where(c == 0, keep, gone), jnp.where(c == 0, gone, keep)], axis=1)
    return (
        o_chunks[0][None],
        dq_chunks[0][None],
        dk_chunks[0][None],
        dv_chunks[0][None],
        weight_grad,
    )


def solution(mesh):
    rows = P("dp", "ctx", None)
    return jax.shard_map(
        per_device,
        mesh=mesh,
        in_specs=(rows,) * 5 + (P("dp", None), P("dp", None)),
        out_specs=(rows,) * 4 + (P(("dp", "ctx"), None),),
        check_vma=False,
    )
```

time: 961 us -> 169 us (0.18)
  waiting for transfers between devices: 638 us -> 61.2 us
  matrix products: 117 us -> 2.28 us
  local copies, waits for them, and re-layouts: 82 us -> 19.5 us
  blocking collectives: 57.1 us -> 0 us
  Pallas kernels: 0 us -> 27.1 us
  starting transfers between devices: 24.7 us -> 49 us
  between operations: 14.1 us -> 0.91 us
    unnamed x2 -> x0, waiting for transfers between devices: 573 us -> none
    dot_general x49 -> x1, matrix products: 117 us -> 2.28 us  [per_device(): jnp.dot(x_all.reshape(NZ * 2 * BLK, wide).T, dv_all.reshape(NZ * 2 * BLK,...]
    all_to_all x3 -> x0, blocking collectives: 57.1 us -> none  [the longest x1 36.5 us: per_device(): lax.all_to_all(out_buf, 'ctx', split_axis=0, concat_axis=1, tiled=True)]
    all_to_all x5 -> x1, waiting for transfers between devices: 64.8 us -> 12.3 us  [per_device(): share = lax.all_to_all(share, ('dp', 'ctx'), 0, 0, axis_index_groups=groups)]
    ppermute x0 -> x20, waiting for transfers between devices: none -> 48.9 us  [the longest x3 23.5 us: earlier(): lax.ppermute(a, 'ctx', [(i + 2 * d, i) for i in range(SLOTS - 2 * d)])]
    ppermute x0 -> x20, starting transfers between devices: none -> 35 us  [the longest x6 11.4 us: along_z(): lax.ppermute(a, 'dp', [(i, i // NZ * NZ + (i + d) % NZ) for i in range(NX...]
    unnamed x19 -> x26, local copies, waits for them, and re-layouts: 35.5 us -> 8.16 us
    pallas_call x0 -> x1, Pallas kernels: none -> 27.1 us  [attention(): pl.pallas_call(attention_kernel, grid_spec=pltpu.PrefetchScalarGridSpec(n...]
  transfers between devices with their start and end apart: 6 -> 21, of which waited for: 6 -> 7; matrix products, arithmetic and copies ran while one was open for 4% -> 13% of each run, Pallas kernels for 0% -> 16%
where the time goes in v1:
time: 169 us
  waiting for transfers between devices  61.2 us (36%)
  starting transfers between devices  49 us (29%)
  Pallas kernels  27.1 us (16%)
  local copies, waits for them, and re-layouts  19.5 us (12%)
  other arithmetic  8.9 us (5%)
  matrix products  2.28 us (1%)
    pallas_call x1, Pallas kernels, attention(): pl.pallas_call(attention_kernel, grid_spec=pltpu.PrefetchScalarGridSpec(n...  27.1 us
    ppermute x3, waiting for transfers between devices, earlier(): lax.ppermute(a, 'ctx', [(i + 2 * d, i) for i in range(SLOTS - 2 * d)])  23.5 us
    ppermute x3, waiting for transfers between devices, later(): lax.ppermute(a, 'ctx', [(i, i + 2 * d) for i in range(SLOTS - 2 * d)])  14.1 us
    all_to_all x1, starting transfers between devices, per_device(): share = lax.all_to_all(share, ('dp', 'ctx'), 0, 0, axis_index_groups=groups)  13.9 us
    all_to_all x1, waiting for transfers between devices, per_device(): share = lax.all_to_all(share, ('dp', 'ctx'), 0, 0, axis_index_groups=groups)  12.3 us
    ppermute x6, starting transfers between devices, along_z(): lax.ppermute(a, 'dp', [(i, i // NZ * NZ + (i + d) % NZ) for i in range(NX...  11.4 us
    ppermute x6, waiting for transfers between devices, along_z(): lax.ppermute(a, 'dp', [(i, i // NZ * NZ + (i + d) % NZ) for i in range(NX...  11.3 us
    ppermute x3, starting transfers between devices, later(): lax.ppermute(a, 'ctx', [(i, i + 2 * d) for i in range(SLOTS - 2 * d)])  10.9 us
  transfers between devices with their start and end apart: 21, of which 7 were waited for; matrix products, arithmetic and copies ran while one was open for 13% of the time, Pallas kernels for 16%

profile of v1, /device:TPU:1, one launch (start us, length us, event | category | flops | bytes accessed | tf_op | source)
XLA Modules:
  0.0 168.9 jit_solution(13139815721007903690)
XLA Ops:
  9.8 1.8 %collective-permute-start.12 = (bf16[128,1024]{0,1:T(8,128)(2,1)S(1)}, bf16[128,1024]{0,1:T(8,128)(2,1)}, u32[]{:S(2)}, u32[]{:S(2)}) collective-permute-start(bf16[128,1024]{0,1:T(8,128)(2,1)S(1)} %bitcast.63), channel_id=1, source_target_pairs={{0,8},{8,16},{16,24},{24,0},{32,40},{40,48},{48,56},{56,32},{64,72... | collective-permute-start | bytes 786440 | tf_op jit(solution)/shard_map/ppermute | solution.py:245
  11.6 3.3 %collective-permute-start.13 = (bf16[128,1024]{0,1:T(8,128)(2,1)S(1)}, bf16[128,1024]{0,1:T(8,128)(2,1)S(1)}, u32[]{:S(2)}, u32[]{:S(2)}) collective-permute-start(bf16[128,1024]{0,1:T(8,128)(2,1)S(1)} %bitcast.62), channel_id=1, source_target_pairs={{0,16},{8,24},{16,0},{24,8},{32,48},{40,56},{48,32},{56,40},{64,80... | collective-permute-start | bytes 786440 | tf_op jit(solution)/shard_map/ppermute | solution.py:245
  16.7 3.3 %collective-permute-done.12 = bf16[128,1024]{0,1:T(8,128)(2,1)} collective-permute-done((bf16[128,1024]{0,1:T(8,128)(2,1)S(1)}, bf16[128,1024]{0,1:T(8,128)(2,1)}, u32[]{:S(2)}, u32[]{:S(2)}) %collective-permute-start.12) | collective-permute-done | bytes 262176 | tf_op jit(solution)/shard_map/ppermute | solution.py:245
  20.0 3.2 %collective-permute-start.3 = (bf16[2,2,128,512]{3,2,1,0:T(8,128)(2,1)S(1)}, bf16[2,2,128,512]{3,2,1,0:T(8,128)(2,1)S(1)}, u32[]{:S(2)}, u32[]{:S(2)}) collective-permute-start(bf16[2,2,128,512]{3,2,1,0:T(8,128)(2,1)S(1)} %pad_maximum_fusion.3.kv0), channel_id=1, source_target_pairs={{0,2},{1,3},{2,4},{3,5},{4,6},{5,7},{8,10},{9,11},{10,12},{11,13},... | collective-permute-start | bytes 1572872 | tf_op jit(solution)/shard_map/ppermute | solution.py:239
  23.2 3.1 %collective-permute-done.13 = bf16[128,1024]{0,1:T(8,128)(2,1)S(1)} collective-permute-done((bf16[128,1024]{0,1:T(8,128)(2,1)S(1)}, bf16[128,1024]{0,1:T(8,128)(2,1)S(1)}, u32[]{:S(2)}, u32[]{:S(2)}) %collective-permute-start.13) | collective-permute-done | bytes 262176 | tf_op jit(solution)/shard_map/ppermute | solution.py:245
  26.4 5.6 %collective-permute-start.4 = (bf16[2,2,128,512]{3,2,1,0:T(8,128)(2,1)S(1)}, bf16[2,2,128,512]{3,2,1,0:T(8,128)(2,1)}, u32[]{:S(2)}, u32[]{:S(2)}) collective-permute-start(bf16[2,2,128,512]{3,2,1,0:T(8,128)(2,1)S(1)} %pad_maximum_fusion.3.kv0), channel_id=1, source_target_pairs={{0,4},{1,5},{2,6},{3,7},{8,12},{9,13},{10,14},{11,15},{16,20},{17,... | collective-permute-start | bytes 1572872 | tf_op jit(solution)/shard_map/ppermute | solution.py:239
  32.7 2.1 %collective-permute-start.5 = (bf16[2,2,128,512]{3,2,1,0:T(8,128)(2,1)S(1)}, bf16[2,2,128,512]{3,2,1,0:T(8,128)(2,1)}, u32[]{:S(2)}, u32[]{:S(2)}) collective-permute-start(bf16[2,2,128,512]{3,2,1,0:T(8,128)(2,1)S(1)} %pad_maximum_fusion.3.kv0), channel_id=1, source_target_pairs={{0,6},{1,7},{8,14},{9,15},{16,22},{17,23},{24,30},{25,31},{32,38},... | collective-permute-start | bytes 1572872 | tf_op jit(solution)/shard_map/ppermute | solution.py:239
  34.9 2.7 %fusion.1 = (bf16[4,1,128,1024]{2,3,0,1:T(8,128)(2,1)}, bf16[4,128,1024]{1,2,0:T(8,128)(2,1)}) fusion(bf16[1,128,1024]{1,2,0:T(8,128)(2,1)} %bitcast.60, bf16[1,128,1024]{1,2,0:T(8,128)(2,1)} %bitcast.59, bf16[1,128,1024]{1,2,0:T(8,128)(2,1)} %bitcast.17, bf16[1,128,1024]{1,2,0:T(8,128)(2,1)S(1)} %bitcast.52), kind=kLoop, calls=%fused_computation.33 | loop fusion | flops 1572864 | bytes 3145728 | tf_op jit(solution)/shard_map/stack | solution.py:285
  38.4 1.6 collective-permute-start.15
  40.1 4.6 %collective-permute-done.4.kv2 = bf16[2,2,128,512]{3,2,1,0:T(8,128)(2,1)} collective-permute-done((bf16[2,2,128,512]{3,2,1,0:T(8,128)(2,1)S(1)}, bf16[2,2,128,512]{3,2,1,0:T(8,128)(2,1)}, u32[]{:S(2)}, u32[]{:S(2)}) %collective-permute-start.4) | collective-permute-done | bytes 524320 | tf_op jit(solution)/shard_map/ppermute | solution.py:239
  44.6 9.5 %collective-permute-done.5.kv3 = bf16[2,2,128,512]{3,2,1,0:T(8,128)(2,1)} collective-permute-done((bf16[2,2,128,512]{3,2,1,0:T(8,128)(2,1)S(1)}, bf16[2,2,128,512]{3,2,1,0:T(8,128)(2,1)}, u32[]{:S(2)}, u32[]{:S(2)}) %collective-permute-start.5) | collective-permute-done | bytes 524320 | tf_op jit(solution)/shard_map/ppermute | solution.py:239
  55.2 27.1 %tree_attention.1 = (bf16[128,8192]{1,0:T(8,128)(2,1)}, bf16[128,4096]{1,0:T(8,128)(2,1)S(1)}, bf16[128,8192]{1,0:T(8,128)(2,1)}, bf16[128,4096]{1,0:T(8,128)(2,...) custom-call(s32[2]{0:T(128)S(1)} %pad_add_fusion.place, ...), custom_call_target="tpu_custom_call" | custom-call | flops 6442450944 | bytes 8388608 | tf_op jit(solution)/shard_map/tree_attention/pallas_call | solution.py:186
  88.8 23.5 %collective-permute-done.10 = bf16[2,2,128,512]{3,2,1,0:T(8,128)(2,1)S(1)} collective-permute-done((bf16[2,2,128,512]{3,2,1,0:T(8,128)(2,1)}, bf16[2,2,128,512]{3,2,1,0:T(8,128)(2,1)S(1)}, u32[]{:S(2)}, u32[]{:S(2)}) %collective-permute-start.10) | collective-permute-done | bytes 524320 | tf_op jit(solution)/shard_map/ppermute | solution.py:242
  113.8 3.1 %collective-permute-start.16 = (bf16[256,512]{1,0:T(8,128)(2,1)S(1)}, bf16[256,512]{1,0:T(8,128)(2,1)}, u32[]{:S(2)}, u32[]{:S(2)}) collective-permute-start(bf16[256,512]{1,0:T(8,128)(2,1)S(1)} %bitcast.55), channel_id=1, source_target_pairs={{0,8},{8,16},{16,24},{24,0},{32,40},{40,48},{48,56},{56,32},{64,72... | collective-permute-start | bytes 786440 | tf_op jit(solution)/shard_map/ppermute | solution.py:245
  116.9 2.5 %collective-permute-start.18 = (bf16[256,512]{1,0:T(8,128)(2,1)S(1)}, bf16[256,512]{1,0:T(8,128)(2,1)}, u32[]{:S(2)}, u32[]{:S(2)}) collective-permute-start(bf16[256,512]{1,0:T(8,128)(2,1)S(1)} %bitcast.57), channel_id=1, source_target_pairs={{0,24},{8,0},{16,8},{24,16},{32,56},{40,32},{48,40},{56,48},{64,88... | collective-permute-start | bytes 786440 | tf_op jit(solution)/shard_map/ppermute | solution.py:245
  119.4 1.7 %pad_maximum_fusion = bf16[4,2,128,1024]{2,3,0,1:T(8,128)(2,1)S(1)} fusion(bf16[4,1,128,1024]{2,3,0,1:T(8,128)(2,1)} %bitcast.23, bf16[4,1,128,1024]{2,3,0,1:T(8,128)(2,1)} %get-tuple-element.21), kind=kLoop, calls=%fused_computation | loop fusion | flops 1048576 | bytes 4194304 | tf_op jit(solution)/shard_map/stack | solution.py:285
  121.1 2.7 %copy.17 = bf16[4,2,128,1024]{3,2,1,0:T(8,128)(2,1)} copy(bf16[4,2,128,1024]{2,3,0,1:T(8,128)(2,1)S(1)} %pad_maximum_fusion) | data formatting | bytes 4194304 | tf_op jit(solution)/shard_map/stack | solution.py:285
  123.9 4.8 %collective-permute-done.16 = bf16[256,512]{1,0:T(8,128)(2,1)} collective-permute-done((bf16[256,512]{1,0:T(8,128)(2,1)S(1)}, bf16[256,512]{1,0:T(8,128)(2,1)}, u32[]{:S(2)}, u32[]{:S(2)}) %collective-permute-start.16) | collective-permute-done | bytes 262176 | tf_op jit(solution)/shard_map/ppermute | solution.py:245
  130.8 2.3 %convolution_convert_fusion = bf16[1024,512]{1,0:T(8,128)(2,1)} fusion(bf16[1024,1024]{1,0:T(8,128)(2,1)S(1)} %bitcast.51, bf16[1024,512]{1,0:T(8,128)(2,1)S(1)} %bitcast.54), kind=kOutput, calls=%fused_computation.2 | convolution fusion | flops 1074266112 | bytes 4194304 | tf_op jit(solution)/shard_map/dot_general | solution.py:287
  133.1 13.9 %all-to-all-start = ((bf16[16,64,512]{2,1,0:T(8,128)(2,1)}), bf16[16,64,512]{2,1,0:T(8,128)(2,1)S(1)}, u32[]{:S(2)}, u32[]{:S(2)}) async-start(bf16[16,64,512]{2,1,0:T(8,128)(2,1)} %bitcast.53), calls=%async_computation | async-start | bytes 2097152 | tf_op jit(solution)/shard_map/all_to_all | solution.py:294
  147.9 2.3 %bitcast_dynamic-update-slice_fusion = bf16[1,128,8192]{2,1,0:T(8,128)(2,1)} fusion(bf16[1,128,8192]{2,1,0:T(8,128)(2,1)} %bitcast.10, s32[]{:T(128)S(6)} %select_n.88, bf16[128,4096]{1,0:T(8,128)(2,1)} %collective-permute-done.7), kind=kLoop, calls=%fused_computation.5 | loop fusion | bytes 2097156 | tf_op jit(solution)/shard_map/dynamic_update_slice | solution.py:267
  150.2 12.3 %all-to-all-done = bf16[16,64,512]{2,1,0:T(8,128)(2,1)S(1)} async-done(((bf16[16,64,512]{2,1,0:T(8,128)(2,1)}), bf16[16,64,512]{2,1,0:T(8,128)(2,1)S(1)}, u32[]{:S(2)}, u32[]{:S(2)}) %all-to-all-start) | async-done | bytes 1048608 | tf_op jit(solution)/shard_map/all_to_all | solution.py:294
  162.7 3.3 %collective-permute-start.19 = (f32[32,512]{1,0:T(8,128)S(1)}, f32[32,512]{1,0:T(8,128)S(1)}, u32[]{:S(2)}, u32[]{:S(2)}) collective-permute-start(f32[32,512]{1,0:T(8,128)S(1)} %constant_dynamic-slice_fusion), channel_id=1, source_target_pairs={{0,1},{1,0},{2,3},{3,2},{4,5},{5,4},{6,7},{7,6},{8,9},{9,8},{10,11... | collective-permute-start | bytes 196616 | tf_op jit(solution)/shard_map/ppermute | solution.py:236
  166.0 2.3 %bitcast_dynamic-update-slice_fusion.1 = bf16[1,128,8192]{2,1,0:T(8,128)(2,1)} fusion(bf16[1,128,8192]{2,1,0:T(8,128)(2,1)} %bitcast.64, s32[]{:T(128)S(6)} %select_n.88, bf16[128,4096]{1,0:T(8,128)(2,1)} %collective-permute-done.6), kind=kLoop, calls=%fused_computation.6 | loop fusion | bytes 2097156 | tf_op jit(solution)/shard_map/dynamic_update_slice | solution.py:266
  (69 shorter events, 25.2 us)
Async XLA Ops:
  3.6 11.3 %collective-permute-start.2 = (bf16[2,128,512]{2,1,0:T(8,128)(2,1)}, bf16[2,128,512]{2,1,0:T(8,128)(2,1)}, u32[]{:S(2)}, u32[]{:S(2)}) collective-permute-start(bf16[2,128,512]{2,1,0:T(8,128)(2,1)} %get-tuple-element.32), channel_id=1, source_target_pairs={{0,1},{1,0},{2,3},{3,2},{4,5},{5,4},{6,7},{7,6},{8,9},{9,8},{10,11... | collective-permute-start | bytes 786440 | tf_op jit(solution)/shard_map/ppermute | solution.py:236
  6.1 48.1 %collective-permute-start = (bf16[128,4096]{1,0:T(8,128)(2,1)}, bf16[128,4096]{1,0:T(8,128)(2,1)}, u32[]{:S(2)}, u32[]{:S(2)}) collective-permute-start(bf16[128,4096]{1,0:T(8,128)(2,1)} %dynamic-slice_bitcast_fusion.1), channel_id=1, source_target_pairs={{0,1},{1,0},{2,3},{3,2},{4,5},{5,4},{6,7},{7,6},{8,9},{9,8},{10,11... | collective-permute-start | bytes 3145736 | tf_op jit(solution)/shard_map/ppermute | solution.py:236
  8.0 46.1 %collective-permute-start.1 = (bf16[128,4096]{1,0:T(8,128)(2,1)}, bf16[128,4096]{1,0:T(8,128)(2,1)}, u32[]{:S(2)}, u32[]{:S(2)}) collective-permute-start(bf16[128,4096]{1,0:T(8,128)(2,1)} %dynamic-slice_bitcast_fusion), channel_id=1, source_target_pairs={{0,1},{1,0},{2,3},{3,2},{4,5},{5,4},{6,7},{7,6},{8,9},{9,8},{10,11... | collective-permute-start | bytes 3145736 | tf_op jit(solution)/shard_map/ppermute | solution.py:236
  9.8 10.2 %collective-permute-start.12 = (bf16[128,1024]{0,1:T(8,128)(2,1)S(1)}, bf16[128,1024]{0,1:T(8,128)(2,1)}, u32[]{:S(2)}, u32[]{:S(2)}) collective-permute-start(bf16[128,1024]{0,1:T(8,128)(2,1)S(1)} %bitcast.63), channel_id=1, source_target_pairs={{0,8},{8,16},{16,24},{24,0},{32,40},{40,48},{48,56},{56,32},{64,72... | collective-permute-start | bytes 786440 | tf_op jit(solution)/shard_map/ppermute | solution.py:245
  11.6 14.8 %collective-permute-start.13 = (bf16[128,1024]{0,1:T(8,128)(2,1)S(1)}, bf16[128,1024]{0,1:T(8,128)(2,1)S(1)}, u32[]{:S(2)}, u32[]{:S(2)}) collective-permute-start(bf16[128,1024]{0,1:T(8,128)(2,1)S(1)} %bitcast.62), channel_id=1, source_target_pairs={{0,16},{8,24},{16,0},{24,8},{32,48},{40,56},{48,32},{56,40},{64,80... | collective-permute-start | bytes 786440 | tf_op jit(solution)/shard_map/ppermute | solution.py:245
  14.9 17.1 %collective-permute-start.14 = (bf16[128,1024]{0,1:T(8,128)(2,1)S(1)}, bf16[128,1024]{0,1:T(8,128)(2,1)S(1)}, u32[]{:S(2)}, u32[]{:S(2)}) collective-permute-start(bf16[128,1024]{0,1:T(8,128)(2,1)S(1)} %bitcast.61), channel_id=1, source_target_pairs={{0,24},{8,0},{16,8},{24,16},{32,56},{40,32},{48,40},{56,48},{64,88... | collective-permute-start | bytes 786440 | tf_op jit(solution)/shard_map/ppermute | solution.py:245
  15.6 38.6 %copy-start.7 = (s32[1,8]{1,0:T(1,128)S(1)}, s32[1,8]{1,0:T(1,128)}, u32[]{:S(2)}) copy-start(s32[1,8]{1,0:T(1,128)} %parents.1) | copy-start | bytes 100
  15.6 38.6 %copy-start.8 = (s32[1,8]{1,0:T(1,128)S(1)}, s32[1,8]{1,0:T(1,128)}, u32[]{:S(2)}) copy-start(s32[1,8]{1,0:T(1,128)} %labels.1) | copy-start | bytes 100
  20.0 17.6 %collective-permute-start.3 = (bf16[2,2,128,512]{3,2,1,0:T(8,128)(2,1)S(1)}, bf16[2,2,128,512]{3,2,1,0:T(8,128)(2,1)S(1)}, u32[]{:S(2)}, u32[]{:S(2)}) collective-permute-start(bf16[2,2,128,512]{3,2,1,0:T(8,128)(2,1)S(1)} %pad_maximum_fusion.3.kv0), channel_id=1, source_target_pairs={{0,2},{1,3},{2,4},{3,5},{4,6},{5,7},{8,10},{9,11},{10,12},{11,13},... | collective-permute-start | bytes 1572872 | tf_op jit(solution)/shard_map/ppermute | solution.py:239
  26.4 18.3 %collective-permute-start.4 = (bf16[2,2,128,512]{3,2,1,0:T(8,128)(2,1)S(1)}, bf16[2,2,128,512]{3,2,1,0:T(8,128)(2,1)}, u32[]{:S(2)}, u32[]{:S(2)}) collective-permute-start(bf16[2,2,128,512]{3,2,1,0:T(8,128)(2,1)S(1)} %pad_maximum_fusion.3.kv0), channel_id=1, source_target_pairs={{0,4},{1,5},{2,6},{3,7},{8,12},{9,13},{10,14},{11,15},{16,20},{17,... | collective-permute-start | bytes 1572872 | tf_op jit(solution)/shard_map/ppermute | solution.py:239
  32.7 21.5 %collective-permute-start.5 = (bf16[2,2,128,512]{3,2,1,0:T(8,128)(2,1)S(1)}, bf16[2,2,128,512]{3,2,1,0:T(8,128)(2,1)}, u32[]{:S(2)}, u32[]{:S(2)}) collective-permute-start(bf16[2,2,128,512]{3,2,1,0:T(8,128)(2,1)S(1)} %pad_maximum_fusion.3.kv0), channel_id=1, source_target_pairs={{0,6},{1,7},{8,14},{9,15},{16,22},{17,23},{24,30},{25,31},{32,38},... | collective-permute-start | bytes 1572872 | tf_op jit(solution)/shard_map/ppermute | solution.py:239
  34.8 19.4 %copy-start.2 = (bf16[1,128,8192]{2,1,0:T(8,128)(2,1)S(1)}, bf16[1,128,8192]{2,1,0:T(8,128)(2,1)}, u32[]{:S(2)}) copy-start(bf16[1,128,8192]{2,1,0:T(8,128)(2,1)} %param.11) | copy-start | bytes 6291460
  38.4 78.5 %collective-permute-start.15 = (bf16[4,128,1024]{1,2,0:T(8,128)(2,1)}, bf16[4,128,1024]{1,2,0:T(8,128)(2,1)}, u32[]{:S(2)}, u32[]{:S(2)}) collective-permute-start(bf16[4,128,1024]{1,2,0:T(8,128)(2,1)} %get-tuple-element.22), channel_id=1, source_target_pairs={{0,1},{1,0},{2,3},{3,2},{4,5},{5,4},{6,7},{7,6},{8,9},{9,8},{10,11... | collective-permute-start | bytes 3145736 | tf_op jit(solution)/shard_map/ppermute | solution.py:236
  84.4 28.0 %collective-permute-start.10 = (bf16[2,2,128,512]{3,2,1,0:T(8,128)(2,1)}, bf16[2,2,128,512]{3,2,1,0:T(8,128)(2,1)S(1)}, u32[]{:S(2)}, u32[]{:S(2)}) collective-permute-start(bf16[2,2,128,512]{3,2,1,0:T(8,128)(2,1)} %get-tuple-element.20), channel_id=1, source_target_pairs={{6,0},{7,1},{14,8},{15,9},{22,16},{23,17},{30,24},{31,25},{38,32},... | collective-permute-start | bytes 1572872 | tf_op jit(solution)/shard_map/ppermute | solution.py:242
  85.6 27.8 %collective-permute-start.8 = (bf16[2,2,128,512]{3,2,1,0:T(8,128)(2,1)}, bf16[2,2,128,512]{3,2,1,0:T(8,128)(2,1)S(1)}, u32[]{:S(2)}, u32[]{:S(2)}) collective-permute-start(bf16[2,2,128,512]{3,2,1,0:T(8,128)(2,1)} %get-tuple-element.18), channel_id=1, source_target_pairs={{2,0},{3,1},{4,2},{5,3},{6,4},{7,5},{10,8},{11,9},{12,10},{13,11},... | collective-permute-start | bytes 1572872 | tf_op jit(solution)/shard_map/ppermute | solution.py:242
  86.9 26.5 %collective-permute-start.9 = (bf16[2,2,128,512]{3,2,1,0:T(8,128)(2,1)}, bf16[2,2,128,512]{3,2,1,0:T(8,128)(2,1)S(1)}, u32[]{:S(2)}, u32[]{:S(2)}) collective-permute-start(bf16[2,2,128,512]{3,2,1,0:T(8,128)(2,1)} %get-tuple-element.19), channel_id=1, source_target_pairs={{4,0},{5,1},{6,2},{7,3},{12,8},{13,9},{14,10},{15,11},{20,16},{21,... | collective-permute-start | bytes 1572872 | tf_op jit(solution)/shard_map/ppermute | solution.py:242
  88.3 59.7 %collective-permute-start.7 = (bf16[128,4096]{1,0:T(8,128)(2,1)}, bf16[128,4096]{1,0:T(8,128)(2,1)}, u32[]{:S(2)}, u32[]{:S(2)}) collective-permute-start(bf16[128,4096]{1,0:T(8,128)(2,1)} %copy-done.4), channel_id=1, source_target_pairs={{0,1},{1,0},{2,3},{3,2},{4,5},{5,4},{6,7},{7,6},{8,9},{9,8},{10,11... | collective-permute-start | bytes 3145736 | tf_op jit(solution)/shard_map/ppermute | solution.py:236
  112.4 53.6 %collective-permute-start.6 = (bf16[128,4096]{1,0:T(8,128)(2,1)}, bf16[128,4096]{1,0:T(8,128)(2,1)}, u32[]{:S(2)}, u32[]{:S(2)}) collective-permute-start(bf16[128,4096]{1,0:T(8,128)(2,1)} %copy-done.3), channel_id=1, source_target_pairs={{0,1},{1,0},{2,3},{3,2},{4,5},{5,4},{6,7},{7,6},{8,9},{9,8},{10,11... | collective-permute-start | bytes 3145736 | tf_op jit(solution)/shard_map/ppermute | solution.py:236
  113.8 14.9 %collective-permute-start.16 = (bf16[256,512]{1,0:T(8,128)(2,1)S(1)}, bf16[256,512]{1,0:T(8,128)(2,1)}, u32[]{:S(2)}, u32[]{:S(2)}) collective-permute-start(bf16[256,512]{1,0:T(8,128)(2,1)S(1)} %bitcast.55), channel_id=1, source_target_pairs={{0,8},{8,16},{16,24},{24,0},{32,40},{40,48},{48,56},{56,32},{64,72... | collective-permute-start | bytes 786440 | tf_op jit(solution)/shard_map/ppermute | solution.py:245
  116.9 12.6 %collective-permute-start.17 = (bf16[256,512]{1,0:T(8,128)(2,1)S(1)}, bf16[256,512]{1,0:T(8,128)(2,1)}, u32[]{:S(2)}, u32[]{:S(2)}) collective-permute-start(bf16[256,512]{1,0:T(8,128)(2,1)S(1)} %bitcast.56), channel_id=1, source_target_pairs={{0,16},{8,24},{16,0},{24,8},{32,48},{40,56},{48,32},{56,40},{64,80... | collective-permute-start | bytes 786440 | tf_op jit(solution)/shard_map/ppermute | solution.py:245
  116.9 12.6 %collective-permute-start.18 = (bf16[256,512]{1,0:T(8,128)(2,1)S(1)}, bf16[256,512]{1,0:T(8,128)(2,1)}, u32[]{:S(2)}, u32[]{:S(2)}) collective-permute-start(bf16[256,512]{1,0:T(8,128)(2,1)S(1)} %bitcast.57), channel_id=1, source_target_pairs={{0,24},{8,0},{16,8},{24,16},{32,56},{40,32},{48,40},{56,48},{64,88... | collective-permute-start | bytes 786440 | tf_op jit(solution)/shard_map/ppermute | solution.py:245
  128.7 18.3 %collective-permute-start.11 = (bf16[2,128,512]{2,1,0:T(8,128)(2,1)S(1)}, bf16[2,128,512]{2,1,0:T(8,128)(2,1)S(1)}, u32[]{:S(2)}, u32[]{:S(2)}) collective-permute-start(bf16[2,128,512]{2,1,0:T(8,128)(2,1)S(1)} %slice_bitcast_fusion), channel_id=1, source_target_pairs={{0,1},{1,0},{2,3},{3,2},{4,5},{5,4},{6,7},{7,6},{8,9},{9,8},{10,11... | collective-permute-start | bytes 786440 | tf_op jit(solution)/shard_map/ppermute | solution.py:236
  133.1 29.4 %all-to-all-start = ((bf16[16,64,512]{2,1,0:T(8,128)(2,1)}), bf16[16,64,512]{2,1,0:T(8,128)(2,1)S(1)}, u32[]{:S(2)}, u32[]{:S(2)}) async-start(bf16[16,64,512]{2,1,0:T(8,128)(2,1)} %bitcast.53), calls=%async_computation | async-start | bytes 2097152 | tf_op jit(solution)/shard_map/all_to_all | solution.py:294
  162.7 5.6 %collective-permute-start.19 = (f32[32,512]{1,0:T(8,128)S(1)}, f32[32,512]{1,0:T(8,128)S(1)}, u32[]{:S(2)}, u32[]{:S(2)}) collective-permute-start(f32[32,512]{1,0:T(8,128)S(1)} %constant_dynamic-slice_fusion), channel_id=1, source_target_pairs={{0,1},{1,0},{2,3},{3,2},{4,5},{5,4},{6,7},{7,6},{8,9},{9,8},{10,11... | collective-permute-start | bytes 196616 | tf_op jit(solution)/shard_map/ppermute | solution.py:236
  (9 other events, 23.4 us)
